TPU v7x, 512 devices: a whole 4x8x8 slice. The times are simulated.
512 devices in a mesh: dp: 64 (over y, x, core), rep: 8 (over z).
Axes of the slice: x: 4, y: 8, z: 8, core: 2. Of those that a mesh axis runs over, the one named last changes fastest.
Arguments:
- grad: bfloat16 [192, 720896], P('rep', 'dp'), parts along dimension 0, may hold values from -170 to 170
- momentum: float32 [192, 720896], P('rep', 'dp'), parts along dimension 0, may hold values from -340 to 340
- owners: int32 [192], P('rep'), parts along dimension 0, may hold values from 0 to 63, as said below
Outputs:
- new_momentum: float32 [192, 720896], P('rep', 'dp'), parts along dimension 0
- update: bfloat16 [192, 720896], P('rep', 'dp'), parts along dimension 0
- owned: bfloat16 [512, 704, 1024], P(('rep', 'dp')), parts along dimension 0
There are 8 independent parts, one for each index of `rep`. A program takes and returns all parts, laid end to end along the dimension named above; each array names one. Nothing has to cross between parts.
Inputs may be any that keep to these rules, and one draw needn't show every extreme that they name: `owners`: no two matrices have the same owner.
All inputs are finite; a program needn't handle non-finite values.
Results may differ from a plain program's by a relative error of at most 0.007.
Values may be sent and summed in bfloat16 or wider, within the bound.
A program may use at most 64 MiB of HBM per device.

v0:
```python
import math

import jax
import jax.numpy as jnp
from jax import lax
from jax.experimental import pallas as pl
from jax.experimental.pallas import tpu as pltpu
from jax.sharding import PartitionSpec as P

R = 704
C = 1024
RP = 768
MATS = 24
N = 64
T = 88
TILES = C // 128
PARTS = ((0, 30), (30, 30), (60, 28))
ROWS = ((0, 240), (240, 240), (480, 224))
MAIN_KIB = 52000
FIXED = 24

MOMENTUM_RATE = 0.95
EPSILON = 1e-07
COEF_A = 3.4445
COEF_B = -4.775
COEF_C = 2.0315
SCALE = 0.2 * math.sqrt(max(R, C))
MESH = pl.DeviceIdType.MESH
NT = (((1,), (1,)), ((), ()))


def ring_offset(u):
    v = 7 - u
    odd = v % 2
    return odd * ((v + 1) // 2) + (1 - odd) * (8 - v // 2)


def fixed_device(d):
    row = d // 3
    return 8 * row + (3 * (d % 3) + 6 * row) % 8


def other_device(row, i):
    return 8 * row + (i + 1 + i // 2 + 6 * row) % 8


def kernel(
    owners_hbm, grad_hbm, momentum_hbm,
    *refs,
):
    new_momentum, update, owned = refs[0:3], refs[3:6], refs[6:9]
    (
        owners, grad, momentum, plan, packed, table, place,
        flat, send, held, x, x1, gram, poly, back, got,
        load_sem, met_sem, send_sem, recv_sem, back_sem, got_sem,
    ) = refs[9:]
    me = lax.axis_index("dp")
    row, col = me // 8, me % 8
    turned = (col + 2 * row) % 8
    is_fixed = turned % 3 == 0
    mine = 3 * row + turned // 3

    def load(i):
        columns = pl.ds(128 * PARTS[i][0], 128 * PARTS[i][1])
        return (
            pltpu.make_async_copy(grad_hbm.at[:, columns], grad.at[:, columns], load_sem.at[2 * i]),
            pltpu.make_async_copy(momentum_hbm.at[:, columns], momentum.at[:, columns], load_sem.at[2 * i + 1]),
        )

    whose = pltpu.make_async_copy(owners_hbm, owners, load_sem.at[2 * len(PARTS)])
    planned = pltpu.make_async_copy(plan, table, load_sem.at[2 * len(PARTS)])
    whose.start()
    for i in range(len(PARTS)):
        for copy in load(i):
            copy.start()

    barrier = pltpu.get_barrier_semaphore()

    def greet(s, c):
        there = 8 * ((row + s) % 8) + col
        pl.semaphore_signal(barrier, inc=1, device_id={"dp": there}, device_id_type=MESH)
        there = 8 * row + (col + s) % 8
        pl.semaphore_signal(barrier, inc=1, device_id={"dp": there}, device_id_type=MESH)
        return c

    lax.fori_loop(1, 8, greet, 0, unroll=True)
    whose.wait()
    lane = lax.broadcasted_iota(jnp.int32, (8, 128), 1)
    matrix = jnp.zeros((8, 128), jnp.int32)
    owning = jnp.zeros((8, 128), jnp.int32)
    for k in range(MATS):
        here = lane == owners[k]
        matrix = jnp.where(here, k, matrix)
        owning = jnp.where(here, 1, owning)
    in_fixed = lambda c: (c == 0) | (c == 3) | (c == 6)
    free = in_fixed((lane + 2 * (lane // 8)) & 7) & (lane < N) & (owning == 0)
    rank = jnp.where(free, 1, 0)
    for shift in (1, 2, 4, 8, 16, 32):
        rank = rank + jnp.where(lane >= shift, pltpu.roll(rank, shift, 1), 0)
    rank = jnp.where(free, rank, 0)
    count = jnp.int32(0)
    for k in range(MATS):
        outside = jnp.where(in_fixed((owners[k] + 2 * (owners[k] // 8)) & 7), 0, 1)
        count = count + outside
        matrix = jnp.where(rank == count * outside + (outside - 1), k, matrix)
    plan[0] = matrix
    plan[1] = owning

    planned.start()

    for i, (first, count) in enumerate(PARTS):
        for copy in load(i):
            copy.wait()

        def step(t, c):
            columns = pl.ds(pl.multiple_of(t * 128, 128), 128)
            g = grad[:, columns].astype(jnp.float32)
            m = MOMENTUM_RATE * momentum[:, columns] + g
            new_momentum[i][:, pl.ds(pl.multiple_of((t - first) * 128, 128), 128)] = m
            n = (g + MOMENTUM_RATE * m).astype(jnp.bfloat16).astype(jnp.float32)
            for kt in range(3):
                flat[pl.ds(pl.multiple_of(kt * 704 + t * 8, 8), 8), :] = n[8 * kt : 8 * kt + 8]
            return c

        lax.fori_loop(first, first + count, step, 0, unroll=2)

    for k in range(MATS):
        packed[k] = flat[pl.ds((k // 8) * 704 + k % 8, T, stride=8), :].astype(jnp.bfloat16)

    planned.wait()
    pl.semaphore_wait(barrier, 14)

    def announce(s, c):
        there = 8 * ((row + s) % 8) + col
        pl.semaphore_signal(met_sem, inc=1, device_id={"dp": there}, device_id_type=MESH)
        return c

    lax.fori_loop(1, 8, announce, 0, unroll=True)

    def deliver(p):
        send[p] = packed[table[0, 0, p]]

        @pl.when(p == me)
        def _():
            pltpu.make_async_copy(send.at[p], held.at[p], recv_sem).start()

        @pl.when(p != me)
        def _():
            pltpu.make_async_remote_copy(
                send.at[p], held.at[me], send_sem, recv_sem, device_id={"dp": p}, device_id_type=MESH
            ).start()

    def to_column(s, c):
        deliver(8 * ((row + ring_offset(s)) % 8) + col)
        return c

    lax.fori_loop(0, 7, to_column, 0)
    pl.semaphore_wait(met_sem, 7)

    def deliver_outside(p):
        @pl.when((p % 8 != col) | (p == me))
        def _():
            deliver(p)

    def to_fixed(s, c):
        there = (row + ring_offset(s % 8)) % 8
        deliver_outside(fixed_device(3 * there + (s // 8 + col) % 3))
        return c

    lax.fori_loop(0, FIXED, to_fixed, 0)

    def to_rest(s, c):
        there = (row + ring_offset(s % 8)) % 8
        deliver_outside(other_device(there, (s // 8 + col) % 5))
        return c

    lax.fori_loop(0, N - FIXED, to_rest, 0)

    def find(k, c):
        where = jnp.int32(0)
        for d in range(FIXED):
            where = jnp.where(table[0, 0, fixed_device(d)] == k, d, where)
        place[k] = where
        return c

    lax.fori_loop(0, MATS, find, 0)

    pltpu.make_async_copy(held, held, recv_sem).wait()

    def unpack(q, total):
        block = held[q].astype(jnp.float32)
        flat[pl.ds(pl.multiple_of(q * T, 8), T), :] = block
        return total + jnp.sum((block * block).reshape(T // 8, 8, 128), axis=0)

    total = lax.fori_loop(0, N, unpack, jnp.zeros((8, 128), jnp.float32), unroll=2)
    inverse = 1.0 / (jnp.sqrt(jnp.sum(total)) + EPSILON)

    def normalize(i, c):
        rows = pl.ds(pl.multiple_of(i * 64, 64), 64)
        for t in range(TILES):
            part = flat[pl.ds(i * 512 + t, 64, stride=8), :]
            x[rows, 128 * t : 128 * t + 128] = (part * inverse).astype(jnp.bfloat16)
        return c

    lax.fori_loop(0, R // 64, normalize, 0)
    x[R:, :] = jnp.zeros((RP - R, C), jnp.bfloat16)

    def polynomial(source):
        @pl.loop(0, 3)
        def _(i):
            rows = pl.ds(pl.multiple_of(i * 256, 256), 256)
            gram[rows, :] = lax.dot_general(
                source[rows, :], source[...], NT, preferred_element_type=jnp.float32
            ).astype(jnp.bfloat16)

        @pl.loop(0, 3)
        def _(i):
            rows = pl.ds(pl.multiple_of(i * 256, 256), 256)
            here = gram[rows, :]
            square = jnp.dot(here, gram[...], preferred_element_type=jnp.float32)
            poly[rows, :] = (COEF_B * here.astype(jnp.float32) + COEF_C * square).astype(jnp.bfloat16)

    polynomial(x)

    @pl.loop(0, 3)
    def _(i):
        rows = pl.ds(pl.multiple_of(i * 256, 256), 256)
        y = COEF_A * x[rows, :].astype(jnp.float32) + jnp.dot(
            poly[rows, :], x[...], preferred_element_type=jnp.float32
        )
        x1[rows, :] = y.astype(jnp.bfloat16)

    polynomial(x1)
    owns = table[1, 0, me] > 0

    for t in range(TILES // 2):
        columns = slice(256 * t, 256 * t + 256)
        z = SCALE * (
            COEF_A * x1[:R, columns].astype(jnp.float32)
            + jnp.dot(poly[:R, :], x1[:, columns], preferred_element_type=jnp.float32)
        )
        z_owned = jnp.where(owns, z, 0.0).astype(jnp.bfloat16)
        for i, (first, count) in enumerate(ROWS):
            owned[i][:, columns] = z_owned[first : first + count]
        for h in range(2):
            flat[pl.ds(2 * t + h, R, stride=8), :] = z[:, 128 * h : 128 * h + 128]

    @pl.when(is_fixed)
    def _():
        def give(s, c):
            p = 8 * ((row + ring_offset(s % 8)) % 8) + (s // 8 + col) % 8
            back[p] = flat[pl.ds(pl.multiple_of(p * T, 8), T), :].astype(jnp.bfloat16)

            @pl.when(p == me)
            def _():
                pltpu.make_async_copy(back.at[p], got.at[mine], got_sem).start()

            @pl.when(p != me)
            def _():
                pltpu.make_async_remote_copy(
                    back.at[p], got.at[mine], back_sem, got_sem, device_id={"dp": p}, device_id_type=MESH
                ).start()

            return c

        lax.fori_loop(0, N, give, 0)

    sent = send.at[pl.ds(0, N - 1)]
    pltpu.make_async_copy(sent, sent, send_sem).wait()
    pltpu.make_async_copy(got, got, got_sem).wait()

    for k in range(MATS):
        flat[pl.ds((k // 8) * 704 + k % 8, T, stride=8), :] = got[place[k]].astype(jnp.float32)

    for i, (first, count) in enumerate(PARTS):

        def write(t, c):
            columns = pl.ds(pl.multiple_of((t - first) * 128, 128), 128)
            parts = [flat[pl.ds(pl.multiple_of(kt * 704 + t * 8, 8), 8), :] for kt in range(3)]
            update[i][:, columns] = jnp.concatenate(parts, axis=0).astype(jnp.bfloat16)
            return c

        lax.fori_loop(first, first + count, write, 0, unroll=2)

    @pl.when(is_fixed)
    def _():
        gone = back.at[pl.ds(0, N - 1)]
        pltpu.make_async_copy(gone, gone, back_sem).wait()


def write_kernel(*refs):
    pieces, (new_momentum, update, owned), sems = refs[:9], refs[9:12], refs[12]
    copies = []
    for i in range(3):
        columns = pl.ds(128 * PARTS[i][0], 128 * PARTS[i][1])
        copies += [
            pltpu.make_async_copy(pieces[6 + i], owned.at[0, pl.ds(*ROWS[i]), :], sems.at[6 + i]),
            pltpu.make_async_copy(pieces[i], new_momentum.at[:, columns], sems.at[i]),
            pltpu.make_async_copy(pieces[3 + i], update.at[:, columns], sems.at[3 + i]),
        ]
    for copy in copies:
        copy.start()
    for copy in copies:
        copy.wait()


def body(grad, momentum, owners):
    hbm = pl.BlockSpec(memory_space=pltpu.HBM)
    vmem = pl.BlockSpec(memory_space=pltpu.VMEM)
    bf16, f32, i32 = jnp.bfloat16, jnp.float32, jnp.int32
    pieces = (
        *(jax.ShapeDtypeStruct((MATS, 128 * count), f32) for _, count in PARTS),
        *(jax.ShapeDtypeStruct((MATS, 128 * count), bf16) for _, count in PARTS),
        *(jax.ShapeDtypeStruct((count, C), bf16) for _, count in ROWS),
    )
    results = pl.pallas_call(
        kernel,
        out_shape=pieces,
        in_specs=[hbm, hbm, hbm],
        out_specs=(vmem,) * 9,
        scratch_shapes=[
            pltpu.SMEM((MATS,), i32),
            pltpu.VMEM(grad.shape, bf16),
            pltpu.VMEM(momentum.shape, f32),
            pltpu.VMEM((2, 8, 128), i32),
            pltpu.VMEM((MATS, T, 128), bf16),
            pltpu.SMEM((2, 8, 128), i32),
            pltpu.SMEM((MATS,), i32),
            pltpu.VMEM((N * T, 128), f32),
            pltpu.VMEM((N, T, 128), bf16),
            pltpu.VMEM((N, T, 128), bf16),
            pltpu.VMEM((RP, C), bf16),
            pltpu.VMEM((RP, C), bf16),
            pltpu.VMEM((RP, RP), bf16),
            pltpu.VMEM((RP, RP), bf16),
            pltpu.VMEM((N, T, 128), bf16),
            pltpu.VMEM((FIXED, T, 128), bf16),
            pltpu.SemaphoreType.DMA((2 * len(PARTS) + 1,)),
            pltpu.SemaphoreType.REGULAR,
            pltpu.SemaphoreType.DMA,
            pltpu.SemaphoreType.DMA,
            pltpu.SemaphoreType.DMA,
            pltpu.SemaphoreType.DMA,
        ],
        compiler_params=pltpu.CompilerParams(
            collective_id=0, has_side_effects=True, vmem_limit_bytes=MAIN_KIB << 10
        ),
    )(owners, grad, momentum)
    return pl.pallas_call(
        write_kernel,
        out_shape=(
            jax.ShapeDtypeStruct(momentum.shape, f32),
            jax.ShapeDtypeStruct(grad.shape, bf16),
            jax.ShapeDtypeStruct((1, R, C), bf16),
        ),
        in_specs=[vmem] * 9,
        out_specs=(hbm, hbm, hbm),
        scratch_shapes=[pltpu.SemaphoreType.DMA((9,))],
        compiler_params=pltpu.CompilerParams(vmem_limit_bytes=4 << 20),
    )(*results)


def solution(mesh):
    return jax.shard_map(
        body,
        mesh=mesh,
        in_specs=(P("rep", "dp"), P("rep", "dp"), P("rep")),
        out_specs=(P("rep", "dp"), P("rep", "dp"), P(("rep", "dp"), None, None)),
        check_vma=False,
    )
```

profile of v0, /device:TPU:11, one launch (start us, length us, event | category | flops | bytes accessed | tf_op | source)
XLA Modules:
  0.0 60.3 jit_solution(4595769090411589473)
XLA Ops:
  0.6 0.0 copy-start
  0.6 0.6 %copy-done = s32[24]{0:T(128)S(1)} copy-done((s32[24]{0:T(128)S(1)}, s32[24]{0:T(128)}, u32[]{:S(2)}) %copy-start) | copy-done | bytes 120
  1.3 57.3 %shard_map.58 = (f32[24,3840]{1,0:T(8,128)S(1)}, f32[24,3840]{1,0:T(8,128)S(1)}, f32[24,3584]{1,0:T(8,128)S(1)}, bf16[24,3840]{1,0:T(8,128)(2,1)S(1)}, bf16[24,3...) custom-call(s32[24]{0:T(128)S(1)} %copy-done, ...), custom_call_target="tpu_custom_call" | custom-call | tf_op jit(solution)/shard_map/pallas_call | solution.py:316
  58.6 1.7 %shard_map.59 = (f32[24,11264]{1,0:T(8,128)}, bf16[24,11264]{1,0:T(8,128)(2,1)}, bf16[1,704,1024]{2,1,0:T(8,128)(2,1)}) custom-call(f32[24,3840]{1,0:T(8,128)S(1)} %get-tuple-element.12.refs_0_, f32[24,3840]{1,0:T(8,128)S(1)} %get-tuple-element.13.refs_1_, f32[24,3584]{1,0:T(8,128)S(1)} %get-tuple-element.14.refs_2_, ...), custom_call_target="tpu_custom_call" | custom-call | tf_op jit(solution)/shard_map/pallas_call | solution.py:349
Async XLA Ops:
  0.6 0.7 %copy-start = (s32[24]{0:T(128)S(1)}, s32[24]{0:T(128)}, u32[]{:S(2)}) copy-start(s32[24]{0:T(128)} %owners_hbm.1) | copy-start | bytes 292
where the time goes:
time: 60.4 us; the launch traced here: 60.3 us
  Pallas kernels  59 us (98%)
  local copies, waits for them, and re-layouts  0.65 us (1%)
  between operations  0.65 us (1%)
    pallas_call x1, Pallas kernels, body(): pl.pallas_call(kernel, out_shape=pieces, in_specs=[hbm, hbm, hbm], out_sp...  57.3 us
    pallas_call x1, Pallas kernels, body(): pl.pallas_call(write_kernel, out_shape=(jax.ShapeDtypeStruct(momentum.sha...  1.7 us

commit v1 on v0

--- a/solution.py
+++ b/solution.py
@@ -17,6 +17,7 @@
 PARTS = ((0, 30), (30, 30), (60, 28))
 ROWS = ((0, 240), (240, 240), (480, 224))
 MAIN_KIB = 52000
+AHEAD = 1
 FIXED = 24
 
 MOMENTUM_RATE = 0.95
@@ -247,8 +248,8 @@
 
     @pl.when(is_fixed)
     def _():
-        def give(s, c):
-            p = 8 * ((row + ring_offset(s % 8)) % 8) + (s // 8 + col) % 8
+        def give(there, v):
+            p = 8 * there + (v + col) % 8
             back[p] = flat[pl.ds(pl.multiple_of(p * T, 8), T), :].astype(jnp.bfloat16)
 
             @pl.when(p == me)
@@ -261,9 +262,23 @@
                     back.at[p], got.at[mine], back_sem, got_sem, device_id={"dp": p}, device_id_type=MESH
                 ).start()
 
-            return c
-
-        lax.fori_loop(0, N, give, 0)
+        def to_early(s, c):
+            give((s + row) % 4, s // 4)
+            return c
+
+        def to_both(s, c):
+            there = (row + ring_offset(s % 8)) % 8
+            early = 1 - there // 4
+            give(there, s // 8 + AHEAD * early)
+            return c
+
+        def to_late(s, c):
+            give(4 + (s + row) % 4, 8 - AHEAD + s // 4)
+            return c
+
+        lax.fori_loop(0, 4 * AHEAD, to_early, 0)
+        lax.fori_loop(0, 8 * (8 - AHEAD), to_both, 0)
+        lax.fori_loop(0, 4 * AHEAD, to_late, 0)
 
     sent = send.at[pl.ds(0, N - 1)]
     pltpu.make_async_copy(sent, sent, send_sem).wait()

time: 60.4 us -> 60 us (level)
  no operation moved by 1% of the time
where the time goes in v1:
time: 60 us; the launch traced here: 59.8 us
  Pallas kernels  58.5 us (98%)
  local copies, waits for them, and re-layouts  0.65 us (1%)
  between operations  0.65 us (1%)
    pallas_call x1, Pallas kernels, body(): pl.pallas_call(kernel, out_shape=pieces, in_specs=[hbm, hbm, hbm], out_sp...  56.8 us
    pallas_call x1, Pallas kernels, body(): pl.pallas_call(write_kernel, out_shape=(jax.ShapeDtypeStruct(momentum.sha...  1.7 us

profile of v1, /device:TPU:11, one launch (start us, length us, event | category | flops | bytes accessed | tf_op | source)
XLA Modules:
  0.0 59.8 jit_solution(10092658474130599136)
XLA Ops:
  0.6 0.0 copy-start
  0.6 0.6 %copy-done = s32[24]{0:T(128)S(1)} copy-done((s32[24]{0:T(128)S(1)}, s32[24]{0:T(128)}, u32[]{:S(2)}) %copy-start) | copy-done | bytes 120
  1.3 56.8 %shard_map.58 = (f32[24,3840]{1,0:T(8,128)S(1)}, f32[24,3840]{1,0:T(8,128)S(1)}, f32[24,3584]{1,0:T(8,128)S(1)}, bf16[24,3840]{1,0:T(8,128)(2,1)S(1)}, bf16[24,3...) custom-call(s32[24]{0:T(128)S(1)} %copy-done, ...), custom_call_target="tpu_custom_call" | custom-call | tf_op jit(solution)/shard_map/pallas_call | solution.py:331
  58.1 1.7 %shard_map.59 = (f32[24,11264]{1,0:T(8,128)}, bf16[24,11264]{1,0:T(8,128)(2,1)}, bf16[1,704,1024]{2,1,0:T(8,128)(2,1)}) custom-call(f32[24,3840]{1,0:T(8,128)S(1)} %get-tuple-element.12.refs_0_, f32[24,3840]{1,0:T(8,128)S(1)} %get-tuple-element.13.refs_1_, f32[24,3584]{1,0:T(8,128)S(1)} %get-tuple-element.14.refs_2_, ...), custom_call_target="tpu_custom_call" | custom-call | tf_op jit(solution)/shard_map/pallas_call | solution.py:364
Async XLA Ops:
  0.6 0.7 %copy-start = (s32[24]{0:T(128)S(1)}, s32[24]{0:T(128)}, u32[]{:S(2)}) copy-start(s32[24]{0:T(128)} %owners_hbm.1) | copy-start | bytes 292

commit v2 on v1

--- a/solution.py
+++ b/solution.py
@@ -341,7 +341,7 @@
             pltpu.VMEM((MATS, T, 128), bf16),
             pltpu.SMEM((2, 8, 128), i32),
             pltpu.SMEM((MATS,), i32),
-            pltpu.VMEM((N * T, 128), f32),
+            pltpu.VMEM((N * T + 8, 128), f32),
             pltpu.VMEM((N, T, 128), bf16),
             pltpu.VMEM((N, T, 128), bf16),
             pltpu.VMEM((RP, C), bf16),

time: 60 us -> 60 us (level)
  no operation moved by 1% of the time
where the time goes in v2:
time: 60 us; the launch traced here: 59.8 us
  Pallas kernels  58.5 us (98%)
  local copies, waits for them, and re-layouts  0.65 us (1%)
  between operations  0.65 us (1%)
    pallas_call x1, Pallas kernels, body(): pl.pallas_call(kernel, out_shape=pieces, in_specs=[hbm, hbm, hbm], out_sp...  56.8 us
    pallas_call x1, Pallas kernels, body(): pl.pallas_call(write_kernel, out_shape=(jax.ShapeDtypeStruct(momentum.sha...  1.7 us

profile of v2, /device:TPU:11, one launch (start us, length us, event | category | flops | bytes accessed | tf_op | source)
XLA Modules:
  0.0 59.8 jit_solution(16727420084131967271)
XLA Ops:
  0.6 0.0 copy-start
  0.6 0.6 %copy-done = s32[24]{0:T(128)S(1)} copy-done((s32[24]{0:T(128)S(1)}, s32[24]{0:T(128)}, u32[]{:S(2)}) %copy-start) | copy-done | bytes 120
  1.3 56.8 %shard_map.58 = (f32[24,3840]{1,0:T(8,128)S(1)}, f32[24,3840]{1,0:T(8,128)S(1)}, f32[24,3584]{1,0:T(8,128)S(1)}, bf16[24,3840]{1,0:T(8,128)(2,1)S(1)}, bf16[24,3...) custom-call(s32[24]{0:T(128)S(1)} %copy-done, ...), custom_call_target="tpu_custom_call" | custom-call | tf_op jit(solution)/shard_map/pallas_call | solution.py:331
  58.1 1.7 %shard_map.59 = (f32[24,11264]{1,0:T(8,128)}, bf16[24,11264]{1,0:T(8,128)(2,1)}, bf16[1,704,1024]{2,1,0:T(8,128)(2,1)}) custom-call(f32[24,3840]{1,0:T(8,128)S(1)} %get-tuple-element.12.refs_0_, f32[24,3840]{1,0:T(8,128)S(1)} %get-tuple-element.13.refs_1_, f32[24,3584]{1,0:T(8,128)S(1)} %get-tuple-element.14.refs_2_, ...), custom_call_target="tpu_custom_call" | custom-call | tf_op jit(solution)/shard_map/pallas_call | solution.py:364
Async XLA Ops:
  0.6 0.7 %copy-start = (s32[24]{0:T(128)S(1)}, s32[24]{0:T(128)}, u32[]{:S(2)}) copy-start(s32[24]{0:T(128)} %owners_hbm.1) | copy-start | bytes 292
